TPU v7x, 32 devices: a whole 2x2x4 slice. The times are simulated.
32 devices in a mesh: inline: 4 (over y, x), xline: 8 (over z, core).
Axes of the slice: x: 2, y: 2, z: 4, core: 2. Of those that a mesh axis runs over, the one named last changes fastest.
Arguments:
- base_volume: float32 [64, 128, 256], P('inline', 'xline'), may hold values from -6 to 6
- vintage_traces: float32 [32768, 256], P(('inline', 'xline')), may hold values from -6 to 6
- dest_device: int32 [32768, 1], P(('inline', 'xline')), may hold values from 0 to 31; in each aligned block of 1024 rows (0 to 1023, 1024 to 2047, ...) at most 64 rows name the same one
- dest_slot: int32 [32768], P(('inline', 'xline')), may hold values from 0 to 255
- vintage_id: int32 [32768], P(('inline', 'xline')), may hold values from 0 to 3
- vintage_gains: float32 [4], replicated, may hold values from 0.5 to 2
- dictionary: bfloat16 [512, 512], replicated, may hold values from -0.09375 to 0.09375
Outputs:
- codes: float32 [16, 32, 64, 512], P('inline', 'xline')
- residual: float32 [64, 128, 256], P('inline', 'xline')
Inputs may be any that keep to these rules, and one draw needn't show every extreme that they name: `dest_device`: among the traces of one device, no tile is named more than 64 times, a bound that some block reaches.
All inputs are finite; a program needn't handle non-finite values.
Results may differ from a plain program's by a relative error of at most 0.0022.
Values may be sent and summed in bfloat16 or wider, within the bound.
A program may use at most 64 MiB of HBM per device.

v0:
```python
import jax
import jax.numpy as jnp
from jax import lax
from jax.sharding import PartitionSpec as P

step_size = 0.25
threshold = 0.02


def passed_along(block, axis, distance):
    devices = range(lax.axis_size(axis))
    route = [(i - distance, i) for i in devices if i - distance in devices]
    return lax.ppermute(block, axis, route)


def shrink_codes(values):
    return values - jnp.clip(values, -threshold, threshold)


def extend_field(field_half):
    beyond_cols = passed_along(field_half[:, :4], "xline", -1)
    widened = jnp.concatenate([field_half, beyond_cols], axis=1)
    beyond_rows = passed_along(widened[:4], "inline", -1)
    return jnp.concatenate([widened, beyond_rows], axis=0)


def correlate(field_half, dict_blocks):
    tile_side, time_len = (field_half.shape[0], field_half.shape[2])
    patch_i, patch_k = (tile_side // 4, time_len // 4)
    extended = jnp.pad(extend_field(field_half), ((0, 0), (0, 0), (0, 4)))
    extended = extended.reshape(patch_i + 1, 4, patch_i + 1, 4, patch_k + 1, 4)
    running = None
    for shift_a in (0, 1):
        for shift_b in (0, 1):
            for shift_c in (0, 1):
                block_piece = extended[
                    shift_a : shift_a + patch_i,
                    :,
                    shift_b : shift_b + patch_i,
                    :,
                    shift_c : shift_c + patch_k,
                    :,
                ]
                partial_sum = jnp.einsum(
                    "iajbkc,abcn->ijkn",
                    block_piece,
                    dict_blocks[shift_a, :, shift_b, :, shift_c, :, :],
                    preferred_element_type=jnp.float32,
                )
                running = partial_sum if running is None else running + partial_sum
    return running


def reconstruct(codes_half, dictionary, time_len):
    patch_i, patch_j, patch_k, atom_count = codes_half.shape
    contrib = jnp.einsum(
        "ijkn,en->ijke", codes_half, dictionary, preferred_element_type=jnp.float32
    )
    contrib = contrib.reshape(patch_i, patch_j, patch_k, 2, 4, 2, 4, 2, 4)
    running = None
    for shift_a in (0, 1):
        for shift_b in (0, 1):
            for shift_c in (0, 1):
                block_piece = contrib[:, :, :, shift_a, :, shift_b, :, shift_c, :].transpose(
                    0, 3, 1, 4, 2, 5
                )
                moved = jnp.pad(
                    block_piece,
                    (
                        (shift_a, 1 - shift_a),
                        (0, 0),
                        (shift_b, 1 - shift_b),
                        (0, 0),
                        (shift_c, 1 - shift_c),
                        (0, 0),
                    ),
                )
                running = moved if running is None else running + moved
    extended = running.reshape((patch_i + 1) * 4, (patch_j + 1) * 4, (patch_k + 1) * 4)[
        :, :, :time_len
    ]
    tile_side = patch_i * 4
    from_rows = passed_along(extended[tile_side:].astype(jnp.bfloat16), "inline", 1).astype(
        jnp.float32
    )
    upper_part = extended[:tile_side].at[:4].add(from_rows)
    from_cols = passed_along(upper_part[:, tile_side:].astype(jnp.bfloat16), "xline", 1).astype(
        jnp.float32
    )
    return upper_part[:, :tile_side].at[:, :4].add(from_cols)


def body(
    base_volume, vintage_traces, dest_device, dest_slot, vintage_id, vintage_gains, dictionary
):
    tile_side, time_len = (base_volume.shape[0], base_volume.shape[2])
    inline_count = lax.axis_size("inline")
    xline_count = lax.axis_size("xline")
    device_count = inline_count * xline_count
    trace_count = vintage_traces.shape[0]
    capacity = 2 * trace_count // device_count
    survey_table = (
        vintage_id[:, None] == jnp.arange(vintage_gains.shape[0], dtype=jnp.int32)[None, :]
    )
    trace_gain = jnp.sum(jnp.where(survey_table, vintage_gains[None, :], 0.0), axis=1)
    weighted = vintage_traces * trace_gain[:, None]
    target = dest_device[:, 0]
    onehot = (target[:, None] == jnp.arange(device_count, dtype=jnp.int32)[None, :]).astype(
        jnp.int32
    )
    rank_in = jnp.sum(jnp.cumsum(onehot, axis=0) * onehot, axis=1) - 1
    place_at = target * capacity + rank_in
    send_traces = (
        jnp.zeros((device_count * capacity, time_len), jnp.float32).at[place_at].set(weighted)
    )
    send_slots = jnp.full((device_count * capacity,), -1, jnp.int32).at[place_at].set(dest_slot)
    got_traces, got_slots = (
        lax.all_to_all(send_traces, ("inline", "xline"), split_axis=0, concat_axis=0, tiled=True),
        lax.all_to_all(send_slots, ("inline", "xline"), split_axis=0, concat_axis=0, tiled=True),
    )
    bin_count = tile_side * tile_side
    safe_slots = jnp.where(got_slots < 0, bin_count, got_slots)
    stack = (
        jnp.zeros((bin_count, time_len), jnp.float32).at[safe_slots].add(got_traces, mode="drop")
    )
    fold = (
        jnp.zeros((bin_count,), jnp.float32)
        .at[safe_slots]
        .add(jnp.ones(safe_slots.shape, jnp.float32), mode="drop")
    )
    merged = (base_volume.reshape(bin_count, time_len) + stack) / (1.0 + fold)[:, None]
    merged = merged.reshape(tile_side, tile_side, time_len)
    dict_blocks = dictionary.reshape(2, 4, 2, 4, 2, 4, dictionary.shape[1])
    first = shrink_codes(step_size * correlate(merged.astype(jnp.bfloat16), dict_blocks))
    recon = reconstruct(first.astype(jnp.bfloat16), dictionary, time_len)
    residual = merged - recon
    codes = shrink_codes(first + step_size * correlate(residual.astype(jnp.bfloat16), dict_blocks))
    return (codes, residual)


def solution(mesh):
    in_specs = (
        P("inline", "xline", None),
        P(("inline", "xline"), None),
        P(("inline", "xline"), None),
        P(("inline", "xline")),
        P(("inline", "xline")),
        P(),
        P(),
    )
    out_specs = (P("inline", "xline", None, None), P("inline", "xline", None))
    return jax.shard_map(body, mesh=mesh, in_specs=in_specs, out_specs=out_specs, check_vma=False)
```

profile of v0, /device:TPU:3, one launch (start us, length us, event | category | flops | bytes accessed | tf_op | source)
XLA Modules:
  0.0 211.8 jit_solution(2628397886783640965)
XLA Ops:
  1.4 9.0 %reduce-window.6 = s32[32,8,128]{2,1,0:T(8,128)S(1)} reduce-window(s32[32,8,128]{2,1,0:T(8,128)S(1)} %fusion.58, s32[]{:T(128)} %constant.78.clone.1), window={size=1x1x128 pad=0_0x0_0x127_0}, to_apply=%region_0.1 | reduce-window | flops 4161536 | bytes 262148 | tf_op jit(solution)/shard_map/reduce-window
  12.3 4.5 %scatter_custom_fusion = s32[2048]{0:T(1024)S(1)} fusion(s32[1024]{0:T(1024)S(1)} %bitcast.326, s32[1024]{0:T(1024)} %param.14, s32[]{:T(128)} %constant.76.clone.1), kind=kCustom, calls=%fused_computation.111 | custom fusion | bytes 8704 | tf_op jit(solution)/shard_map/scatter | solution.py:116
  17.5 6.4 %all-to-all-start = ((s32[32,64,1]{1,2,0:T(1,128)}), s32[32,64,1]{1,2,0:T(1,128)S(1)}, u32[]{:S(2)}, u32[]{:S(2)}) async-start(s32[32,64,1]{1,2,0:T(1,128)} %bitcast.7), calls=%async_computation | async-start | bytes 32768 | tf_op jit(solution)/shard_map/all_to_all | solution.py:119
  24.7 6.7 %scatter_custom_fusion.1 = f32[2048,256]{1,0:T(8,128)} fusion(s32[1024]{0:T(1024)S(1)} %bitcast.327, f32[1024,256]{1,0:T(8,128)S(1)} %copy-done.4, f32[]{:T(128)} %constant.81.clone.1, f32[1024]{0:T(1024)S(1)} %select_reduce_fusion), kind=kCustom, calls=%fused_computation.57 | custom fusion | flops 262144 | bytes 3149828 | tf_op jit(solution)/shard_map/scatter | solution.py:114
  31.5 5.8 %all-to-all-start.1 = ((f32[32,64,256]{2,1,0:T(8,128)}), f32[32,64,256]{2,1,0:T(8,128)S(1)}, u32[]{:S(2)}, u32[]{:S(2)}) async-start(f32[32,64,256]{2,1,0:T(8,128)} %bitcast.316), calls=%async_computation.1 | async-start | bytes 4194304 | tf_op jit(solution)/shard_map/all_to_all | solution.py:118
  38.6 14.7 %scatter_custom_fusion.3 = f32[256]{0:T(256)S(1)} fusion(s32[2048]{0:T(1024)S(1)} %bitcast.322, f32[2048]{0:T(1024)S(1)} %broadcast.152, f32[]{:T(128)} %constant.82.clone.1), kind=kCustom, calls=%fused_computation.114 | custom fusion | flops 2048 | bytes 1028 | tf_op jit(solution)/shard_map/scatter-add | solution.py:129
  53.3 33.1 %all-to-all-done.1 = f32[32,64,256]{2,1,0:T(8,128)S(1)} async-done(((f32[32,64,256]{2,1,0:T(8,128)}), f32[32,64,256]{2,1,0:T(8,128)S(1)}, u32[]{:S(2)}, u32[]{:S(2)}) %all-to-all-start.1) | async-done | bytes 2097184 | tf_op jit(solution)/shard_map/all_to_all | solution.py:118
  86.4 11.7 %scatter_fusion = f32[256,256]{1,0:T(8,128)S(1)} fusion(f32[256,256]{1,0:T(8,128)S(1)} %bitcast.313, s32[2048]{0:T(1024)S(1)} %bitcast.323, f32[2048,256]{1,0:T(8,128)S(1)} %bitcast.315), kind=kCustom, calls=%fused_computation.2 | custom fusion | flops 524288 | bytes 6299648 | tf_op jit(solution)/shard_map/scatter-add | solution.py:124
  100.1 3.3 %collective-permute-done = bf16[16,4,256]{2,1,0:T(4,128)(2,1)S(1)} collective-permute-done((bf16[16,4,256]{2,1,0:T(4,128)(2,1)S(1)}, bf16[16,4,256]{2,1,0:T(4,128)(2,1)S(1)}, u32[]{:S(2)}, u32[]{:S(2)}) %collective-permute-start) | collective-permute-done | bytes 32800 | tf_op jit(solution)/shard_map/ppermute | solution.py:13
  103.5 2.5 %collective-permute-start.1 = (bf16[4,20,256]{2,1,0:T(8,128)(2,1)S(1)}, bf16[4,20,256]{2,1,0:T(8,128)(2,1)S(1)}, u32[]{:S(2)}, u32[]{:S(2)}) collective-permute-start(bf16[4,20,256]{2,1,0:T(8,128)(2,1)S(1)} %pad_maximum_fusion.1), channel_id=1, source_target_pairs={{8,0},{16,8},{24,16},{9,1},{17,9},{25,17},{10,2},{18,10},{26,18},{... | collective-permute-start | bytes 122888 | tf_op jit(solution)/shard_map/ppermute | solution.py:13
  106.1 3.1 %collective-permute-done.1 = bf16[4,20,256]{2,1,0:T(8,128)(2,1)S(1)} collective-permute-done((bf16[4,20,256]{2,1,0:T(8,128)(2,1)S(1)}, bf16[4,20,256]{2,1,0:T(8,128)(2,1)S(1)}, u32[]{:S(2)}, u32[]{:S(2)}) %collective-permute-start.1) | collective-permute-done | bytes 40992 | tf_op jit(solution)/shard_map/ppermute | solution.py:13
  109.2 6.3 %reshape.150 = bf16[5,4,5,4,65,4]{5,4,3,2,1,0:T(8,128)(2,1)} reshape(bf16[20,20,260]{2,1,0:T(8,128)(2,1)S(1)} %fusion.53) | data formatting | bytes 416000 | tf_op jit(solution)/shard_map/reshape | solution.py:31
  115.6 3.5 %fusion.18 = f32[4,4,64,512,1,1]{3,2,5,1,4,0:T(8,128)S(1)} fusion(bf16[5,4,5,4,65,4]{5,4,3,2,1,0:T(8,128)(2,1)} %reshape.150, bf16[2,4,2,4,2,4,512]{6,5,4,3,2,1,0:T(4,128)(2,1)S(1)} %reshape.151), kind=kOutput, calls=%fused_computation.22 | convolution fusion | flops 67108864 | bytes 6356992 | tf_op jit(solution)/shard_map/iajbkc,abcn->ijkn/dot_general | solution.py:44
  128.3 14.9 %clamp_subtract_fusion.1 = f32[4,4,64,512]{3,2,1,0:T(8,128)S(1)} fusion(f32[4,4,64,512,1,1]{3,2,5,1,4,0:T(8,128)S(1)} %fusion.18, f32[4,4,64,512,1,1]{3,2,5,1,4,0:T(8,128)S(1)} %fusion.20, f32[4,4,64,512,1,1]{3,2,5,1,4,0:T(8,128)S(1)} %fusion.22, f32[4,4,64,512,1,1]{3,2,5,1,4,0:T(8,128)S(1)} %fusion.24, f32[4,4,64,512,1,1]{3,2,5,1,4,0:T(8,128)S(1)} %fusion.26, ...), kind=kOutput, calls=%fused_computation.37 | convolution fusion | flops 72351744 | bytes 21037056 | tf_op jit(solution)/shard_map/iajbkc,abcn->ijkn/dot_general | solution.py:44
  146.9 8.7 %copy.115 = f32[5,4,5,4,65,4]{5,4,3,2,1,0:T(8,128)} copy(f32[5,4,5,4,65,4]{4,5,3,1,2,0:T(4,128)S(1)} %pad_add_fusion) | data formatting | bytes 832000 | tf_op jit(solution)/shard_map/add | solution.py:78
  155.5 8.6 %reshape.153 = f32[20,20,260]{2,1,0:T(8,128)S(1)} reshape(f32[5,4,5,4,65,4]{5,4,3,2,1,0:T(8,128)} %copy.115) | data formatting | bytes 832000 | tf_op jit(solution)/shard_map/reshape | solution.py:79
  166.4 2.6 %collective-permute-done.2 = bf16[4,20,256]{2,1,0:T(8,128)(2,1)S(1)} collective-permute-done((bf16[4,20,256]{2,1,0:T(8,128)(2,1)S(1)}, bf16[4,20,256]{2,1,0:T(8,128)(2,1)S(1)}, u32[]{:S(2)}, u32[]{:S(2)}) %collective-permute-start.2) | collective-permute-done | bytes 40992 | tf_op jit(solution)/shard_map/ppermute | solution.py:13
  169.0 4.2 %collective-permute-start.3 = (bf16[16,4,256]{2,1,0:T(4,128)(2,1)S(1)}, bf16[16,4,256]{2,1,0:T(4,128)(2,1)S(1)}, u32[]{:S(2)}, u32[]{:S(2)}) collective-permute-start(bf16[16,4,256]{2,1,0:T(4,128)(2,1)S(1)} %slice.352), channel_id=1, source_target_pairs={{0,1},{1,2},{2,3},{3,4},{4,5},{5,6},{6,7},{8,9},{9,10},{10,11},{11... | collective-permute-start | bytes 98312 | tf_op jit(solution)/shard_map/ppermute | solution.py:13
  176.9 3.9 %collective-permute-done.4 = bf16[16,4,256]{2,1,0:T(4,128)(2,1)S(1)} collective-permute-done((bf16[16,4,256]{2,1,0:T(4,128)(2,1)S(1)}, bf16[16,4,256]{2,1,0:T(4,128)(2,1)S(1)}, u32[]{:S(2)}, u32[]{:S(2)}) %collective-permute-start.4) | collective-permute-done | bytes 32800 | tf_op jit(solution)/shard_map/ppermute | solution.py:13
  182.8 3.8 %collective-permute-done.5 = bf16[4,20,256]{2,1,0:T(8,128)(2,1)S(1)} collective-permute-done((bf16[4,20,256]{2,1,0:T(8,128)(2,1)S(1)}, bf16[4,20,256]{2,1,0:T(8,128)(2,1)S(1)}, u32[]{:S(2)}, u32[]{:S(2)}) %collective-permute-start.5) | collective-permute-done | bytes 40992 | tf_op jit(solution)/shard_map/ppermute | solution.py:13
  186.6 6.1 %reshape.154 = bf16[5,4,5,4,65,4]{5,4,3,2,1,0:T(8,128)(2,1)} reshape(bf16[20,20,260]{2,1,0:T(8,128)(2,1)S(1)} %fusion.55) | data formatting | bytes 416000 | tf_op jit(solution)/shard_map/reshape | solution.py:31
  192.7 3.5 %fusion.2 = f32[4,4,64,512,1,1]{3,2,5,1,4,0:T(8,128)S(1)} fusion(bf16[5,4,5,4,65,4]{5,4,3,2,1,0:T(8,128)(2,1)} %reshape.154, bf16[2,4,2,4,2,4,512]{6,5,4,3,2,1,0:T(4,128)(2,1)S(1)} %copy-done.6), kind=kOutput, calls=%fused_computation.6 | convolution fusion | flops 67108864 | bytes 6356992 | tf_op jit(solution)/shard_map/iajbkc,abcn->ijkn/dot_general | solution.py:44
  204.3 2.5 %fusion.14 = f32[4,4,64,512,1,1]{3,2,5,1,4,0:T(8,128)} fusion(bf16[5,4,5,4,65,4]{5,4,3,2,1,0:T(8,128)(2,1)S(1)} %copy-done.1, bf16[2,4,2,4,2,4,512]{6,5,4,3,2,1,0:T(4,128)(2,1)S(1)} %copy-done.6), kind=kOutput, calls=%fused_computation.18 | convolution fusion | flops 67108864 | bytes 6356992 | tf_op jit(solution)/shard_map/iajbkc,abcn->ijkn/dot_general | solution.py:44
  206.8 4.8 %clamp_subtract_fusion = f32[4,4,64,512]{3,2,1,0:T(8,128)} fusion(f32[4,4,64,512]{3,2,1,0:T(8,128)S(1)} %clamp_subtract_fusion.1, f32[4,4,64,512,1,1]{3,2,5,1,4,0:T(8,128)S(1)} %fusion.2, f32[4,4,64,512,1,1]{3,2,5,1,4,0:T(8,128)S(1)} %fusion.4, f32[4,4,64,512,1,1]{3,2,5,1,4,0:T(8,128)S(1)} %fusion.6, f32[4,4,64,512,1,1]{3,2,5,1,4,0:T(8,128)S(1)} %fusion.8, ...), kind=kOutput, calls=%fused_computation.36 | convolution fusion | flops 72876032 | bytes 23134208 | tf_op jit(solution)/shard_map/iajbkc,abcn->ijkn/dot_general | solution.py:44
  (67 shorter events, 36.5 us)
Async XLA Ops:
  0.6 24.1 %copy-start.4 = (f32[1024,256]{1,0:T(8,128)S(1)}, f32[1024,256]{1,0:T(8,128)}, u32[]{:S(2)}) copy-start(f32[1024,256]{1,0:T(8,128)} %param.12) | copy-start | bytes 3145732
  17.5 14.0 %all-to-all-start = ((s32[32,64,1]{1,2,0:T(1,128)}), s32[32,64,1]{1,2,0:T(1,128)S(1)}, u32[]{:S(2)}, u32[]{:S(2)}) async-start(s32[32,64,1]{1,2,0:T(1,128)} %bitcast.7), calls=%async_computation | async-start | bytes 32768 | tf_op jit(solution)/shard_map/all_to_all | solution.py:119
  31.5 54.9 %copy-start = (f32[16,16,256]{2,1,0:T(8,128)S(1)}, f32[16,16,256]{2,1,0:T(8,128)}, u32[]{:S(2)}) copy-start(f32[16,16,256]{2,1,0:T(8,128)} %param.11) | copy-start | bytes 786436
  31.5 54.9 %all-to-all-start.1 = ((f32[32,64,256]{2,1,0:T(8,128)}), f32[32,64,256]{2,1,0:T(8,128)S(1)}, u32[]{:S(2)}, u32[]{:S(2)}) async-start(f32[32,64,256]{2,1,0:T(8,128)} %bitcast.316), calls=%async_computation.1 | async-start | bytes 4194304 | tf_op jit(solution)/shard_map/all_to_all | solution.py:118
  86.4 19.6 %copy-start.3 = (bf16[512,512]{1,0:T(8,128)(2,1)S(1)}, bf16[512,512]{1,0:T(8,128)(2,1)}, u32[]{:S(2)}) copy-start(bf16[512,512]{1,0:T(8,128)(2,1)} %param.17) | copy-start | bytes 1572868
  98.2 5.2 %collective-permute-start = (bf16[16,4,256]{2,1,0:T(4,128)(2,1)S(1)}, bf16[16,4,256]{2,1,0:T(4,128)(2,1)S(1)}, u32[]{:S(2)}, u32[]{:S(2)}) collective-permute-start(bf16[16,4,256]{2,1,0:T(4,128)(2,1)S(1)} %slice.235), channel_id=1, source_target_pairs={{1,0},{2,1},{3,2},{4,3},{5,4},{6,5},{7,6},{9,8},{10,9},{11,10},{12... | collective-permute-start | bytes 98312 | tf_op jit(solution)/shard_map/ppermute | solution.py:13
  103.5 5.7 %collective-permute-start.1 = (bf16[4,20,256]{2,1,0:T(8,128)(2,1)S(1)}, bf16[4,20,256]{2,1,0:T(8,128)(2,1)S(1)}, u32[]{:S(2)}, u32[]{:S(2)}) collective-permute-start(bf16[4,20,256]{2,1,0:T(8,128)(2,1)S(1)} %pad_maximum_fusion.1), channel_id=1, source_target_pairs={{8,0},{16,8},{24,16},{9,1},{17,9},{25,17},{10,2},{18,10},{26,18},{... | collective-permute-start | bytes 122888 | tf_op jit(solution)/shard_map/ppermute | solution.py:13
  106.1 21.1 %copy-start.5 = (bf16[2,4,2,4,2,4,512]{6,5,4,3,2,1,0:T(4,128)(2,1)}, bf16[2,4,2,4,2,4,512]{6,5,4,3,2,1,0:T(4,128)(2,1)S(1)}, u32[]{:S(2)}) copy-start(bf16[2,4,2,4,2,4,512]{6,5,4,3,2,1,0:T(4,128)(2,1)S(1)} %reshape.151) | copy-start | bytes 1572868
  115.6 4.4 %copy-start.2 = (bf16[5,4,5,4,65,4]{5,4,3,2,1,0:T(8,128)(2,1)S(1)}, bf16[5,4,5,4,65,4]{5,4,3,2,1,0:T(8,128)(2,1)}, u32[]{:S(2)}) copy-start(bf16[5,4,5,4,65,4]{5,4,3,2,1,0:T(8,128)(2,1)} %reshape.150) | copy-start | bytes 624004
  164.1 4.8 %collective-permute-start.2 = (bf16[4,20,256]{2,1,0:T(8,128)(2,1)S(1)}, bf16[4,20,256]{2,1,0:T(8,128)(2,1)S(1)}, u32[]{:S(2)}, u32[]{:S(2)}) collective-permute-start(bf16[4,20,256]{2,1,0:T(8,128)(2,1)S(1)} %slice.351), channel_id=1, source_target_pairs={{0,8},{8,16},{16,24},{1,9},{9,17},{17,25},{2,10},{10,18},{18,26},{... | collective-permute-start | bytes 122888 | tf_op jit(solution)/shard_map/ppermute | solution.py:13
  169.0 5.2 %collective-permute-start.3 = (bf16[16,4,256]{2,1,0:T(4,128)(2,1)S(1)}, bf16[16,4,256]{2,1,0:T(4,128)(2,1)S(1)}, u32[]{:S(2)}, u32[]{:S(2)}) collective-permute-start(bf16[16,4,256]{2,1,0:T(4,128)(2,1)S(1)} %slice.352), channel_id=1, source_target_pairs={{0,1},{1,2},{2,3},{3,4},{4,5},{5,6},{6,7},{8,9},{9,10},{10,11},{11... | collective-permute-start | bytes 98312 | tf_op jit(solution)/shard_map/ppermute | solution.py:13
  175.0 5.8 %collective-permute-start.4 = (bf16[16,4,256]{2,1,0:T(4,128)(2,1)S(1)}, bf16[16,4,256]{2,1,0:T(4,128)(2,1)S(1)}, u32[]{:S(2)}, u32[]{:S(2)}) collective-permute-start(bf16[16,4,256]{2,1,0:T(4,128)(2,1)S(1)} %slice.266), channel_id=1, source_target_pairs={{1,0},{2,1},{3,2},{4,3},{5,4},{6,5},{7,6},{9,8},{10,9},{11,10},{12... | collective-permute-start | bytes 98312 | tf_op jit(solution)/shard_map/ppermute | solution.py:13
  180.8 5.7 %collective-permute-start.5 = (bf16[4,20,256]{2,1,0:T(8,128)(2,1)S(1)}, bf16[4,20,256]{2,1,0:T(8,128)(2,1)S(1)}, u32[]{:S(2)}, u32[]{:S(2)}) collective-permute-start(bf16[4,20,256]{2,1,0:T(8,128)(2,1)S(1)} %pad_maximum_fusion), channel_id=1, source_target_pairs={{8,0},{16,8},{24,16},{9,1},{17,9},{25,17},{10,2},{18,10},{26,18},{... | collective-permute-start | bytes 122888 | tf_op jit(solution)/shard_map/ppermute | solution.py:13
  186.6 6.1 %copy-start.6 = (bf16[2,4,2,4,2,4,512]{6,5,4,3,2,1,0:T(4,128)(2,1)S(1)}, bf16[2,4,2,4,2,4,512]{6,5,4,3,2,1,0:T(4,128)(2,1)}, u32[]{:S(2)}) copy-start(bf16[2,4,2,4,2,4,512]{6,5,4,3,2,1,0:T(4,128)(2,1)} %copy-done.5) | copy-start | bytes 1572868
  192.7 4.4 %copy-start.1 = (bf16[5,4,5,4,65,4]{5,4,3,2,1,0:T(8,128)(2,1)S(1)}, bf16[5,4,5,4,65,4]{5,4,3,2,1,0:T(8,128)(2,1)}, u32[]{:S(2)}) copy-start(bf16[5,4,5,4,65,4]{5,4,3,2,1,0:T(8,128)(2,1)} %reshape.154) | copy-start | bytes 624004
where the time goes:
time: 213 us; the launch traced here: 212 us
  waiting for transfers between devices  50.8 us (24%)
  other arithmetic  48.1 us (23%)
  matrix products  46.1 us (22%)
  local copies, waits for them, and re-layouts  38.8 us (18%)
  starting transfers between devices  26.9 us (13%)
    dot_general x16, matrix products, correlate(): jnp.einsum('iajbkc,abcn->ijkn', block_piece, dict_blocks[shift_a, :, shif...  44.9 us
    all_to_all x1, waiting for transfers between devices, body(): lax.all_to_all(send_traces, ('inline', 'xline'), split_axis=0, concat_axi...  33.1 us
    ppermute x6, waiting for transfers between devices, passed_along(): return lax.ppermute(block, axis, route)  17.7 us
    scatter-add x1, other arithmetic, body(): fold = jnp.zeros((bin_count,), jnp.float32).at[safe_slots].add(jnp.ones(s...  14.7 us
    ppermute x6, starting transfers between devices, passed_along(): return lax.ppermute(block, axis, route)  14.6 us
    reshape x2, local copies, waits for them, and re-layouts, correlate(): extended = extended.reshape(patch_i + 1, 4, patch_i + 1, 4, patch_k + 1, 4)  12.4 us
    scatter-add x1, other arithmetic, body(): jnp.zeros((bin_count, time_len), jnp.float32).at[safe_slots]  11.7 us
    another operation x3, other arithmetic  9.15 us
  transfers between devices with their start and end apart: 8, of which 7 were waited for; matrix products, arithmetic and copies ran while one was open for 11% of the time, Pallas kernels for 0%

commit v1 on v0

v1 whole, which is shorter than its diff:
```python
import functools
import jax
import jax.numpy as jnp
from jax import lax
from jax.experimental import pallas as pl
from jax.experimental.pallas import tpu as pltpu
from jax.sharding import PartitionSpec as P

step_size = 0.25
threshold = 0.02
WIRE = jnp.int16
FULL = 32768.0
MESH = pl.DeviceIdType.MESH
F32, BF16 = jnp.float32, jnp.bfloat16


def shrink_codes(values):
    return values - jnp.clip(values, -threshold, threshold)


def iota(shape, dim):
    return lax.broadcasted_iota(jnp.int32, shape, dim)


def split_half(x):
    hi = x.astype(BF16)
    return hi, (x - hi.astype(F32)).astype(BF16)


def exchange_kernel(nx, n, cap, w_ref, tgt_ref, slot_ref, unit_ref, base_ref, out_ref, whl, rank, grid_sel,
                    meta_out, meta_in, send, got, acc, fold, basep, moves,
                    send_sem, recv_sem, msend_sem, mrecv_sem):
    me = lax.axis_index("inline") * nx + lax.axis_index("xline")
    side, time_len = base_ref.shape[0], base_ref.shape[2]
    blocks = side // 4
    bins = side * side
    traces = w_ref.shape[0]
    q = 256 // cap
    chunks = n // q

    def where_is(p):
        return (p // nx, p % nx)

    barrier = pltpu.get_barrier_semaphore()

    @pl.loop(1, n)
    def _(off):
        pl.semaphore_signal(barrier, inc=1, device_id=where_is((me + off) % n), device_id_type=MESH)

    hi, lo = split_half(w_ref[...])
    whl[:, :time_len] = hi
    whl[:, time_len:] = lo
    tri = (iota((128, 128), 0) <= iota((128, 128), 1)).astype(F32).astype(BF16)
    base_count = jnp.zeros((n, 1), F32)
    for b in range(traces // 128):
        mine = tgt_ref[:, b * 128:(b + 1) * 128] == iota((n, 128), 0)
        one = jnp.where(mine, 1.0, 0.0)
        cum = jnp.dot(one.astype(BF16), tri, preferred_element_type=F32) + base_count
        rank[:, b * 128:(b + 1) * 128] = jnp.where(mine, cum - 1.0, -1.0)
        base_count = base_count + jnp.sum(one, axis=1, keepdims=True)
    slot = slot_ref[...]
    r, c = slot // side, slot % side
    binned = ((r // 4) * blocks + c // 4) * 16 + (r % 4) * 4 + c % 4
    first_row = iota((16, traces), 0) == 0
    about = jnp.where(first_row, (binned + 1).astype(F32), unit_ref[...]).astype(BF16)
    my_q = me % q
    lane_from, lane_to = iota((256, 256), 0), iota((256, 256), 1)
    for i in range(q):
        move = (lane_from - my_q * cap == lane_to - i * cap) & (lane_to // cap == i)
        moves[i] = jnp.where(move, 1.0, 0.0).astype(BF16)
    for bi in range(blocks):
        for bj in range(blocks):
            for a in range(4):
                at = (bi * blocks + bj) * 16 + a * 4
                basep[at:at + 4, :] = base_ref[4 * bi + a, 4 * bj:4 * bj + 4, :]
    acc[...] = jnp.zeros_like(acc)
    fold[...] = jnp.zeros_like(fold)

    @pl.loop(0, chunks)
    def _(step):
        ch = (me // q + 1 + step) % chunks
        want = iota((cap, traces), 0).astype(F32)
        for i in range(q):
            row = rank[pl.ds(ch * q + i, 1), :]
            grid_sel[i * cap:(i + 1) * cap, :] = jnp.where(row == want, 1.0, 0.0).astype(BF16)
        sel = grid_sel[...]
        picked = jnp.dot(sel, whl[...], preferred_element_type=F32)
        packed = (picked[:, :time_len] + picked[:, time_len:]).astype(jnp.int32).astype(WIRE)
        names = lax.dot_general(about, sel, (((1,), (1,)), ((), ())), preferred_element_type=F32)
        meta_out[ch] = names[0:2, :]
        for i in range(q):
            send[ch * q + i] = packed[i * cap:(i + 1) * cap, :]

        @pl.when(step == 0)
        def _():
            pl.semaphore_wait(barrier, n - 1)

        for i in range(q):
            p = ch * q + i

            @pl.when(p != me)
            def _():
                pltpu.make_async_remote_copy(
                    meta_out.at[ch], meta_in.at[me], msend_sem, mrecv_sem.at[me],
                    device_id=where_is(p), device_id_type=MESH).start()
                pltpu.make_async_remote_copy(
                    send.at[p], got.at[me], send_sem, recv_sem.at[me],
                    device_id=where_is(p), device_id_type=MESH).start()

            @pl.when(p == me)
            def _():
                meta_in[me] = meta_out[ch]
                got[me] = send[p]

    @pl.loop(0, chunks)
    def _(step):
        ch = (me // q + chunks - 1 - step + chunks) % chunks
        names = jnp.zeros((16, 256), F32)
        for i in range(q):
            src = ch * q + i

            @pl.when(src != me)
            def _():
                pltpu.make_async_remote_copy(
                    meta_out.at[0], meta_in.at[src], msend_sem, mrecv_sem.at[src],
                    device_id=where_is(src), device_id_type=MESH).wait_recv()
                pltpu.make_async_remote_copy(
                    send.at[src], got.at[src], send_sem, recv_sem.at[src],
                    device_id=where_is(src), device_id_type=MESH).wait_recv()

            both = meta_in[src]
            row = jnp.where(iota((16, 256), 0) == 0, both[0:1, :], both[1:2, :]).astype(BF16)
            names = names + jnp.dot(row, moves[i], preferred_element_type=F32)
        hit = jnp.where(names[0:1, :] == (iota((bins, 256), 0) + 1).astype(F32), 1.0, 0.0)
        rows = got[pl.ds(ch * q, q)].astype(jnp.int32).astype(F32).reshape(256, time_len)
        hi, lo = split_half(rows)
        half = (hit * names[1:2, :]).astype(BF16)
        acc[...] += jnp.dot(half, hi, preferred_element_type=F32) + jnp.dot(half, lo, preferred_element_type=F32)
        fold[...] += hit

    count = jnp.sum(fold[...], axis=1, keepdims=True)
    out_ref[...] = (basep[...] + acc[...] * (1.0 / FULL)) / (1.0 + count)
    all_data = send.at[pl.ds(0, n - 1)]
    pltpu.make_async_copy(all_data, got.at[pl.ds(0, n - 1)], send_sem).wait()
    pltpu.make_async_copy(meta_in.at[pl.ds(0, n - 1)], meta_in.at[pl.ds(0, n - 1)], msend_sem).wait()


def patches_of(v_ref, i, blocks):
    rows = []
    for j in range(blocks):
        rows.append(jnp.concatenate(
            [v_ref[i + sa, j + sb] for sa in (0, 1) for sb in (0, 1)], axis=1))
    return jnp.concatenate(rows, axis=0)


def fold_time(x):
    rolled = pltpu.roll(x, 64, 1)
    rolled = pltpu.roll(rolled, 1, 0)
    return x + jnp.where(iota(x.shape, 0) == 0, 0.0, rolled)


def widen_time(x):
    ahead = pltpu.roll(pltpu.roll(x, 64, 1), x.shape[0] - 1, 0)
    ahead = jnp.where(iota(x.shape, 0) == x.shape[0] - 1, 0.0, ahead)
    return jnp.where(iota(x.shape, 1) < 64, x, ahead)


def ista_kernel(ni, nx, m_ref, d_ref, v1_ref, v2_ref, res_ref, tsc, cube, spread, out_half,
                from_row, from_col, from_cor, ssem, rsem):
    mi, mx = lax.axis_index("inline"), lax.axis_index("xline")
    blocks = v1_ref.shape[0] - 1
    kt = v1_ref.shape[2]
    cells, time_len = m_ref.shape
    barrier = pltpu.get_barrier_semaphore()

    def greet(di, dx):
        ok = (mi + di >= 0) & (mi + di < ni) & (mx + dx >= 0) & (mx + dx < nx)

        @pl.when(ok)
        def _():
            pl.semaphore_signal(barrier, inc=1, device_id=(mi + di, mx + dx), device_id_type=MESH)

    around = [(-1, 0), (0, -1), (-1, -1), (1, 0), (0, 1), (1, 1)]
    for di, dx in around:
        greet(di, dx)

    has_prev = [mi > 0, mx > 0, (mi > 0) & (mx > 0)]
    has_next = [mi < ni - 1, mx < nx - 1, (mi < ni - 1) & (mx < nx - 1)]
    steps = [(1, 0), (0, 1), (1, 1)]

    def halo_copies(v_ref, slot):
        pairs = [(v_ref.at[0, pl.ds(0, blocks)], v_ref.at[blocks, pl.ds(0, blocks)]),
                 (v_ref.at[pl.ds(0, blocks), 0], v_ref.at[pl.ds(0, blocks), blocks]),
                 (v_ref.at[0, 0], v_ref.at[blocks, blocks])]
        return [pltpu.make_async_remote_copy(
            src, dst, ssem.at[slot, m], rsem.at[slot, m],
            device_id=(mi - steps[m][0], mx - steps[m][1]), device_id_type=MESH)
            for m, (src, dst) in enumerate(pairs)]

    def clear_edges(v_ref):
        blank = jnp.zeros((kt, 128), BF16)

        @pl.when(mi == ni - 1)
        def _():
            for j in range(blocks + 1):
                v_ref[blocks, j] = blank

        @pl.when(mx == nx - 1)
        def _():
            for i in range(blocks + 1):
                v_ref[i, blocks] = blank

    def run(copies, guards, what):
        for copy, guard in zip(copies, guards):
            @pl.when(guard)
            def _():
                getattr(copy, what)()

    lane = iota((kt, 128), 1) // 16
    turned = m_ref[...].T
    for col in range(cells // 128):
        tsc[col, time_len:, :] = jnp.zeros((8, 128), F32)
        tsc[col, :time_len, :] = turned[:, col * 128:(col + 1) * 128]
    clear_edges(v1_ref)
    clear_edges(v2_ref)
    for col in range(cells // 128):
        parts = [tsc[col, pl.ds(g, kt, stride=4), :] for g in range(8)]
        for e in range(8):
            b = col * 8 + e
            v = parts[e]
            for g in range(8):
                if g != e:
                    v = jnp.where(lane == g, pltpu.roll(parts[g], ((g - e) * 16) % 128, 1), v)
            cube[b] = v
            v1_ref[b // blocks, b % blocks] = v.astype(BF16)
    up, down = (mi > 0).astype(jnp.int32), (mi < ni - 1).astype(jnp.int32)
    west, east = (mx > 0).astype(jnp.int32), (mx < nx - 1).astype(jnp.int32)
    pl.semaphore_wait(barrier, up + down + west + east + up * west + down * east)
    sends = halo_copies(v1_ref, 0)
    run(sends, has_prev, "start")
    run(sends, has_next, "wait_recv")

    for i in range(blocks + 1):
        for j in range(blocks + 1):
            spread[i, j] = jnp.zeros((kt, 128), F32)
    for i in range(blocks):
        first = shrink_codes(step_size * jnp.dot(patches_of(v1_ref, i, blocks), d_ref[...],
                                                 preferred_element_type=F32))
        back = lax.dot_general(first.astype(BF16), d_ref[...], (((1,), (1,)), ((), ())),
                               preferred_element_type=F32)
        for j in range(blocks):
            for sa in (0, 1):
                for sb in (0, 1):
                    g = (2 * sa + sb) * 128
                    spread[i + sa, j + sb] += back[j * kt:(j + 1) * kt, g:g + 128]
    for j in range(blocks):
        out_half[j] = fold_time(spread[blocks, j]).astype(BF16)
        out_half[blocks + j] = fold_time(spread[j, blocks]).astype(BF16)
    out_half[2 * blocks] = fold_time(spread[blocks, blocks]).astype(BF16)
    ends = [(out_half.at[pl.ds(0, blocks)], from_row), (out_half.at[pl.ds(blocks, blocks)], from_col),
            (out_half.at[2 * blocks], from_cor)]
    terms = [pltpu.make_async_remote_copy(
        src, dst, ssem.at[1, m], rsem.at[1, m],
        device_id=(mi + steps[m][0], mx + steps[m][1]), device_id_type=MESH)
        for m, (src, dst) in enumerate(ends)]
    run(terms, has_next, "start")

    for guard, ref in zip(has_prev, (from_row, from_col, from_cor)):
        @pl.when(jnp.logical_not(guard))
        def _():
            ref[...] = jnp.zeros_like(ref)

    def finish(i, j, more):
        b = i * blocks + j
        whole = fold_time(spread[i, j])
        for term in more:
            whole = whole + term.astype(F32)
        left = cube[b] - whole
        cube[b] = left
        v2_ref[i, j] = widen_time(left).astype(BF16)

    for i in range(1, blocks):
        for j in range(1, blocks):
            finish(i, j, [])
    run(terms, has_prev, "wait_recv")
    finish(0, 0, [from_row[0], from_col[0], from_cor[...]])
    for j in range(1, blocks):
        finish(0, j, [from_row[j]])
        finish(j, 0, [from_col[j]])
    last = halo_copies(v2_ref, 2)
    run(last, has_prev, "start")

    for col in range(cells // 128):
        parts = [cube[col * 8 + e] for e in range(8)]
        for s in range(4):
            v = parts[s]
            for e in range(8):
                if e != s:
                    v = jnp.where(lane == e, pltpu.roll(parts[e], ((e - s) * 16) % 128, 1), v)
            tsc[col, pl.ds(s, kt, stride=4), :] = v
    flat = jnp.concatenate([tsc[col, :time_len, :] for col in range(cells // 128)], axis=1).T
    for bi in range(blocks):
        for bj in range(blocks):
            for a in range(4):
                at = (bi * blocks + bj) * 16 + a * 4
                res_ref[4 * bi + a, 4 * bj:4 * bj + 4, :] = flat[at:at + 4, :]
    run(last, has_next, "wait_recv")
    run(sends, has_prev, "wait_send")
    run(terms, has_next, "wait_send")
    run(last, has_prev, "wait_send")


def codes_kernel(v1_ref, v2_ref, d_ref, out_ref):
    blocks = v1_ref.shape[0] - 1
    i = pl.program_id(0)
    first = shrink_codes(step_size * jnp.dot(patches_of(v1_ref, i, blocks), d_ref[...],
                                             preferred_element_type=F32))
    again = step_size * jnp.dot(patches_of(v2_ref, i, blocks), d_ref[...], preferred_element_type=F32)
    out_ref[...] = shrink_codes(first + again).reshape(out_ref.shape)


def body(ni, nx, base_volume, vintage_traces, dest_device, dest_slot, vintage_id, vintage_gains, dictionary):
    side, time_len = base_volume.shape[0], base_volume.shape[2]
    n = ni * nx
    traces = vintage_traces.shape[0]
    cap = 2 * traces // n
    blocks, kt, cells = side // 4, time_len // 4, side * side
    atoms = dictionary.shape[1]
    table = vintage_id[:, None] == jnp.arange(vintage_gains.shape[0], dtype=jnp.int32)[None, :]
    gain = jnp.sum(jnp.where(table, vintage_gains[None, :], 0.0), axis=1)
    weighted = vintage_traces * gain[:, None]
    largest = jnp.max(jnp.abs(weighted), axis=1)
    unit = jnp.full((traces,), 16.0, F32)
    for power in range(3, -31, -1):
        unit = jnp.where(largest < 2.0 ** power, 2.0 ** power, unit)
    whole_steps = jnp.clip(jnp.round(weighted * (FULL / unit)[:, None]), 1.0 - FULL, FULL - 1.0)
    ordered = dictionary.reshape(2, 4, 2, 4, 8, atoms).transpose(0, 2, 4, 1, 3, 5).reshape(512, atoms)
    vmem = pl.BlockSpec(memory_space=pltpu.VMEM)
    dma = pltpu.SemaphoreType.DMA
    merged = pl.pallas_call(
        functools.partial(exchange_kernel, nx, n, cap),
        out_shape=jax.ShapeDtypeStruct((cells, time_len), F32),
        in_specs=[vmem] * 5, out_specs=vmem,
        scratch_shapes=[
            pltpu.VMEM((traces, 2 * time_len), BF16), pltpu.VMEM((n, traces), F32),
            pltpu.VMEM((256, traces), BF16), pltpu.VMEM((n * cap // 256, 2, 256), F32),
            pltpu.VMEM((n, 2, 256), F32), pltpu.VMEM((n, cap, time_len), WIRE),
            pltpu.VMEM((n, cap, time_len), WIRE), pltpu.VMEM((cells, time_len), F32),
            pltpu.VMEM((cells, 256), F32), pltpu.VMEM((cells, time_len), F32),
            pltpu.VMEM((256 // cap, 256, 256), BF16),
            dma, dma((n,)), dma, dma((n,))],
        compiler_params=pltpu.CompilerParams(collective_id=0, has_side_effects=True,
                                             vmem_limit_bytes=40 << 20),
        name="exchange",
    )(whole_steps, dest_device.reshape(1, traces), dest_slot.reshape(1, traces), unit.reshape(1, traces), base_volume)
    halo = (blocks + 1, blocks + 1, kt, 128)
    v1, v2, residual = pl.pallas_call(
        functools.partial(ista_kernel, ni, nx),
        out_shape=(jax.ShapeDtypeStruct(halo, BF16), jax.ShapeDtypeStruct(halo, BF16),
                   jax.ShapeDtypeStruct(base_volume.shape, F32)),
        in_specs=[vmem] * 2, out_specs=(vmem,) * 3,
        scratch_shapes=[
            pltpu.VMEM((cells // 128, time_len + 8, 128), F32), pltpu.VMEM((blocks * blocks, kt, 128), F32),
            pltpu.VMEM(halo, F32), pltpu.VMEM((2 * blocks + 1, kt, 128), BF16),
            pltpu.VMEM((blocks, kt, 128), BF16), pltpu.VMEM((blocks, kt, 128), BF16),
            pltpu.VMEM((kt, 128), BF16), dma((3, 3)), dma((3, 3))],
        compiler_params=pltpu.CompilerParams(collective_id=1, has_side_effects=True,
                                             vmem_limit_bytes=40 << 20),
        name="ista",
    )(merged, ordered)
    whole = lambda *shape: pl.BlockSpec(shape, lambda i: (0,) * len(shape))
    codes = pl.pallas_call(
        codes_kernel,
        grid=(blocks,),
        out_shape=jax.ShapeDtypeStruct((blocks, blocks, kt, atoms), F32),
        in_specs=[whole(*halo), whole(*halo), whole(512, atoms)],
        out_specs=pl.BlockSpec((1, blocks, kt, atoms), lambda i: (i, 0, 0, 0)),
        compiler_params=pltpu.CompilerParams(vmem_limit_bytes=40 << 20),
        name="codes",
    )(v1, v2, ordered)
    return codes, residual


def solution(mesh):
    in_specs = (
        P("inline", "xline", None),
        P(("inline", "xline"), None),
        P(("inline", "xline"), None),
        P(("inline", "xline")),
        P(("inline", "xline")),
        P(),
        P(),
    )
    out_specs = (P("inline", "xline", None, None), P("inline", "xline", None))
    return jax.shard_map(functools.partial(body, mesh.shape["inline"], mesh.shape["xline"]),
                         mesh=mesh, in_specs=in_specs, out_specs=out_specs, check_vma=False)
```

time: 213 us -> 57.3 us (0.27)
  waiting for transfers between devices: 50.8 us -> 0 us
  Pallas kernels: 0 us -> 50.6 us
  matrix products: 46.1 us -> 0 us
  other arithmetic: 48.1 us -> 2.92 us
  local copies, waits for them, and re-layouts: 38.8 us -> 2.2 us
  starting transfers between devices: 26.9 us -> 0 us
    pallas_call x0 -> x3, Pallas kernels: none -> 50.6 us  [the longest x1 31 us: body(): pl.pallas_call(functools.partial(exchange_kernel, nx, n, cap), out_shape=...]
    dot_general x17 -> x0, matrix products: 46.1 us -> none  [the longest x16 44.9 us: correlate(): jnp.einsum('iajbkc,abcn->ijkn', block_piece, dict_blocks[shift_a, :, shif...]
    all_to_all x2 -> x0, waiting for transfers between devices: 33.1 us -> none  [the longest x1 33.1 us: body(): lax.all_to_all(send_traces, ('inline', 'xline'), split_axis=0, concat_axi...]
    scatter-add x4 -> x0, other arithmetic: 26.4 us -> none  [the longest x1 14.7 us: body(): fold = jnp.zeros((bin_count,), jnp.float32).at[safe_slots].add(jnp.ones(s...]
    reshape x4 -> x2, local copies, waits for them, and re-layouts: 21.1 us -> 1.48 us  [body(): dictionary.reshape(2, 4, 2, 4, 8, atoms).transpose(0, 2, 4, 1, 3, 5)]
    ppermute x6 -> x0, waiting for transfers between devices: 17.7 us -> none  [passed_along(): return lax.ppermute(block, axis, route)]
    ppermute x6 -> x0, starting transfers between devices: 14.6 us -> none  [passed_along(): return lax.ppermute(block, axis, route)]
    all_to_all x2 -> x0, starting transfers between devices: 12.3 us -> none  [the longest x1 6.44 us: body(): lax.all_to_all(send_slots, ('inline', 'xline'), split_axis=0, concat_axis...]
  transfers between devices with their start and end apart: 8 -> 0, of which waited for: 7 -> 0; matrix products, arithmetic and copies ran while one was open for 11% -> 0% of each run, Pallas kernels for 0% -> 0%
where the time goes in v1:
time: 57.3 us; the launch traced here: 56.5 us
  Pallas kernels  50.6 us (88%)
  other arithmetic  2.92 us (5%)
  local copies, waits for them, and re-layouts  2.2 us (4%)
  between operations  0.75 us (1%)
    pallas_call x1, Pallas kernels, body(): pl.pallas_call(functools.partial(exchange_kernel, nx, n, cap), out_shape=...  31 us
    pallas_call x1, Pallas kernels, body(): pl.pallas_call(functools.partial(ista_kernel, ni, nx), out_shape=(jax.Sha...  16.8 us
    pallas_call x1, Pallas kernels, body(): pl.pallas_call(codes_kernel, grid=(blocks,), out_shape=jax.ShapeDtypeStru...  2.94 us
    reduce_max x1, other arithmetic, body(): largest = jnp.max(jnp.abs(weighted), axis=1)  1.59 us
    reshape x2, local copies, waits for them, and re-layouts, body(): dictionary.reshape(2, 4, 2, 4, 8, atoms).transpose(0, 2, 4, 1, 3, 5)  1.48 us

profile of v1, /device:TPU:3, one launch (start us, length us, event | category | flops | bytes accessed | tf_op | source)
XLA Modules:
  0.0 56.5 jit_solution(3893057499190173995)
XLA Ops:
  0.6 0.0 copy-start.3
  0.6 0.9 %select_reduce_fusion = f32[1024]{0:T(1024)S(1)} fusion(f32[4]{0:T(128)} %param.12, s32[1024]{0:T(1024)} %param.11), kind=kLoop, calls=%fused_computation.3 | loop fusion | flops 11264 | bytes 8208 | tf_op jit(solution)/shard_map/reduce_sum | solution.py:330
  1.5 1.6 %abs_reduce_fusion = f32[1024]{0:T(1024)S(1)} fusion(f32[1024,256]{1,0:T(8,128)} %param.8, f32[1024]{0:T(1024)S(1)} %select_reduce_fusion), kind=kLoop, calls=%fused_computation.1 | loop fusion | flops 785408 | bytes 1056768 | tf_op jit(solution)/shard_map/reduce_max | solution.py:332
  3.1 0.1 reshape_select_fusion.18.unit_ref
  3.2 0.0 copy-start
  3.3 0.0 copy-start.1
  3.3 0.0 copy-start.2
  3.3 1.4 %copy.12 = bf16[2,4,2,4,8,512]{5,3,1,4,2,0:T(4,128)(2,1)S(1)} copy(bf16[2,4,2,4,8,512]{5,4,3,2,1,0:T(8,128)(2,1)} %bitcast.10) | data formatting | bytes 1048576 | tf_op jit(solution)/shard_map/reshape | solution.py:337
  4.6 0.1 reshape.377.d_ref
  4.8 0.0 copy-done.3
  4.8 0.3 round-nearest-even_clamp_fusion.w_ref
  5.1 0.0 copy-done
  5.1 0.0 copy-done.1
  5.1 0.0 copy-done.2
  5.2 31.0 %exchange.1.m_ref = f32[256,256]{1,0:T(8,128)S(1)} custom-call(f32[1024,256]{1,0:T(8,128)S(1)} %round-nearest-even_clamp_fusion.w_ref, s32[1,1024]{1,0:T(1,128)S(1)} %bitcast.7, s32[1,1024]{1,0:T(1,128)S(1)} %bitcast.8, f32[1,1024]{1,0:T(1,128)S(1)} %reshape_select_fusion.18.unit_ref, f32[16,16,256]{2,1,0:T(8,128)S(1)} %copy-done), custom_call_target="tpu_custom_call" | custom-call | tf_op jit(solution)/shard_map/exchange/pallas_call | solution.py:340
  36.1 16.8 %ista.1 = (bf16[5,5,64,128]{3,2,1,0:T(8,128)(2,1)S(1)}, bf16[5,5,64,128]{3,2,1,0:T(8,128)(2,1)S(1)}, f32[16,16,256]{2,1,0:T(8,128)S(1)}) custom-call(f32[256,256]{1,0:T(8,128)S(1)} %exchange.1.m_ref, bf16[512,512]{1,0:T(8,128)(2,1)S(1)} %reshape.377.d_ref), custom_call_target="tpu_custom_call" | custom-call | tf_op jit(solution)/shard_map/ista/pallas_call | solution.py:357
  52.9 2.9 %codes.1 = f32[4,4,64,512]{3,2,1,0:T(8,128)} custom-call(bf16[5,5,64,128]{3,2,1,0:T(8,128)(2,1)S(1)} %get-tuple-element.5.v1_ref, bf16[5,5,64,128]{3,2,1,0:T(8,128)(2,1)S(1)} %get-tuple-element.6.v2_ref, bf16[512,512]{1,0:T(8,128)(2,1)S(1)} %reshape.377.d_ref), custom_call_target="tpu_custom_call" | custom-call | tf_op jit(solution)/shard_map/codes/pallas_call | solution.py:372
  55.8 0.7 %copy.14 = f32[16,16,256]{2,1,0:T(8,128)} copy(f32[16,16,256]{2,1,0:T(8,128)S(1)} %get-tuple-element.32) | data formatting | bytes 524288
  (1 shorter events, 0.0 us)
Async XLA Ops:
  0.6 4.1 %copy-start.3 = (f32[1024,256]{1,0:T(8,128)S(1)}, f32[1024,256]{1,0:T(8,128)}, u32[]{:S(2)}) copy-start(f32[1024,256]{1,0:T(8,128)} %param.8) | copy-start | bytes 3145732
  3.2 1.9 %copy-start = (f32[16,16,256]{2,1,0:T(8,128)S(1)}, f32[16,16,256]{2,1,0:T(8,128)}, u32[]{:S(2)}) copy-start(f32[16,16,256]{2,1,0:T(8,128)} %base_ref.1) | copy-start | bytes 786436
  3.3 1.9 %copy-start.1 = (s32[1024,1]{0,1:T(1,128)S(1)}, s32[1024,1]{0,1:T(1,128)}, u32[]{:S(2)}) copy-start(s32[1024,1]{0,1:T(1,128)} %param.9) | copy-start | bytes 12292
  3.3 1.9 %copy-start.2 = (s32[1024]{0:T(1024)S(1)}, s32[1024]{0:T(1024)}, u32[]{:S(2)}) copy-start(s32[1024]{0:T(1024)} %param.10) | copy-start | bytes 12292

commit v2 on v1

--- a/solution.py
+++ b/solution.py
@@ -27,7 +27,7 @@
     return hi, (x - hi.astype(F32)).astype(BF16)
 
 
-def exchange_kernel(nx, n, cap, w_ref, tgt_ref, slot_ref, unit_ref, base_ref, out_ref, whl, rank, grid_sel,
+def exchange(while_waiting, nx, n, cap, w_ref, tgt_ref, slot_ref, unit_ref, base_ref, d_in, out_ref, d_ref, whl, rank, grid_sel,
                     meta_out, meta_in, send, got, acc, fold, basep, moves,
                     send_sem, recv_sem, msend_sem, mrecv_sem):
     me = lax.axis_index("inline") * nx + lax.axis_index("xline")
@@ -112,6 +112,13 @@
                 meta_in[me] = meta_out[ch]
                 got[me] = send[p]
 
+    rows_of, cols_of = iota((512, 512), 0), iota((512, 512), 1)
+    wanted = ((rows_of // 256) * 256 + (rows_of % 16) // 4 * 64 + (rows_of // 128 % 2) * 32
+              + (rows_of % 4) * 8 + rows_of // 16 % 8)
+    d_ref[...] = jnp.dot(jnp.where(wanted == cols_of, 1.0, 0.0).astype(BF16), d_in[...],
+                         preferred_element_type=F32).astype(BF16)
+    while_waiting()
+
     @pl.loop(0, chunks)
     def _(step):
         ch = (me // q + chunks - 1 - step + chunks) % chunks
@@ -140,6 +147,9 @@
 
     count = jnp.sum(fold[...], axis=1, keepdims=True)
     out_ref[...] = (basep[...] + acc[...] * (1.0 / FULL)) / (1.0 + count)
+
+
+def exchange_end(n, send, got, meta_in, send_sem, msend_sem):
     all_data = send.at[pl.ds(0, n - 1)]
     pltpu.make_async_copy(all_data, got.at[pl.ds(0, n - 1)], send_sem).wait()
     pltpu.make_async_copy(meta_in.at[pl.ds(0, n - 1)], meta_in.at[pl.ds(0, n - 1)], msend_sem).wait()
@@ -165,25 +175,15 @@
     return jnp.where(iota(x.shape, 1) < 64, x, ahead)
 
 
-def ista_kernel(ni, nx, m_ref, d_ref, v1_ref, v2_ref, res_ref, tsc, cube, spread, out_half,
-                from_row, from_col, from_cor, ssem, rsem):
+def main_kernel(ni, nx, cap, w_ref, tgt_ref, slot_ref, unit_ref, base_ref, d_in,
+                d_ref, v1_ref, v2_ref, res_ref,
+                m_ref, whl, rank, grid_sel, meta_out, meta_in, send, got, acc, fold, basep, moves,
+                send_sem, recv_sem, msend_sem, mrecv_sem,
+                tsc, cube, spread, out_half, from_row, from_col, from_cor, ssem, rsem):
     mi, mx = lax.axis_index("inline"), lax.axis_index("xline")
     blocks = v1_ref.shape[0] - 1
     kt = v1_ref.shape[2]
     cells, time_len = m_ref.shape
-    barrier = pltpu.get_barrier_semaphore()
-
-    def greet(di, dx):
-        ok = (mi + di >= 0) & (mi + di < ni) & (mx + dx >= 0) & (mx + dx < nx)
-
-        @pl.when(ok)
-        def _():
-            pl.semaphore_signal(barrier, inc=1, device_id=(mi + di, mx + dx), device_id_type=MESH)
-
-    around = [(-1, 0), (0, -1), (-1, -1), (1, 0), (0, 1), (1, 1)]
-    for di, dx in around:
-        greet(di, dx)
-
     has_prev = [mi > 0, mx > 0, (mi > 0) & (mx > 0)]
     has_next = [mi < ni - 1, mx < nx - 1, (mi < ni - 1) & (mx < nx - 1)]
     steps = [(1, 0), (0, 1), (1, 1)]
@@ -216,13 +216,25 @@
             def _():
                 getattr(copy, what)()
 
+    def while_waiting():
+        clear_edges(v1_ref)
+        clear_edges(v2_ref)
+        for col in range(cells // 128):
+            tsc[col, time_len:, :] = jnp.zeros((8, 128), F32)
+        spread[...] = jnp.zeros_like(spread)
+        for guard, ref in zip(has_prev, (from_row, from_col, from_cor)):
+            @pl.when(jnp.logical_not(guard))
+            def _():
+                ref[...] = jnp.zeros_like(ref)
+
+    exchange(while_waiting, nx, ni * nx, cap, w_ref, tgt_ref, slot_ref, unit_ref, base_ref, d_in, m_ref, d_ref,
+             whl, rank, grid_sel, meta_out, meta_in, send, got, acc, fold, basep, moves,
+             send_sem, recv_sem, msend_sem, mrecv_sem)
+
     lane = iota((kt, 128), 1) // 16
     turned = m_ref[...].T
     for col in range(cells // 128):
-        tsc[col, time_len:, :] = jnp.zeros((8, 128), F32)
         tsc[col, :time_len, :] = turned[:, col * 128:(col + 1) * 128]
-    clear_edges(v1_ref)
-    clear_edges(v2_ref)
     for col in range(cells // 128):
         parts = [tsc[col, pl.ds(g, kt, stride=4), :] for g in range(8)]
         for e in range(8):
@@ -233,16 +245,10 @@
                     v = jnp.where(lane == g, pltpu.roll(parts[g], ((g - e) * 16) % 128, 1), v)
             cube[b] = v
             v1_ref[b // blocks, b % blocks] = v.astype(BF16)
-    up, down = (mi > 0).astype(jnp.int32), (mi < ni - 1).astype(jnp.int32)
-    west, east = (mx > 0).astype(jnp.int32), (mx < nx - 1).astype(jnp.int32)
-    pl.semaphore_wait(barrier, up + down + west + east + up * west + down * east)
     sends = halo_copies(v1_ref, 0)
     run(sends, has_prev, "start")
     run(sends, has_next, "wait_recv")
 
-    for i in range(blocks + 1):
-        for j in range(blocks + 1):
-            spread[i, j] = jnp.zeros((kt, 128), F32)
     for i in range(blocks):
         first = shrink_codes(step_size * jnp.dot(patches_of(v1_ref, i, blocks), d_ref[...],
                                                  preferred_element_type=F32))
@@ -265,11 +271,6 @@
         for m, (src, dst) in enumerate(ends)]
     run(terms, has_next, "start")
 
-    for guard, ref in zip(has_prev, (from_row, from_col, from_cor)):
-        @pl.when(jnp.logical_not(guard))
-        def _():
-            ref[...] = jnp.zeros_like(ref)
-
     def finish(i, j, more):
         b = i * blocks + j
         whole = fold_time(spread[i, j])
@@ -308,14 +309,16 @@
     run(sends, has_prev, "wait_send")
     run(terms, has_next, "wait_send")
     run(last, has_prev, "wait_send")
-
-
-def codes_kernel(v1_ref, v2_ref, d_ref, out_ref):
+    exchange_end(ni * nx, send, got, meta_in, send_sem, msend_sem)
+
+
+def codes_kernel(v1_ref, v2_ref, d_ref, held_ref, out_ref, res_ref):
     blocks = v1_ref.shape[0] - 1
     i = pl.program_id(0)
     first = shrink_codes(step_size * jnp.dot(patches_of(v1_ref, i, blocks), d_ref[...],
                                              preferred_element_type=F32))
     again = step_size * jnp.dot(patches_of(v2_ref, i, blocks), d_ref[...], preferred_element_type=F32)
+    res_ref[...] = held_ref[...]
     out_ref[...] = shrink_codes(first + again).reshape(out_ref.shape)
 
 
@@ -334,50 +337,45 @@
     for power in range(3, -31, -1):
         unit = jnp.where(largest < 2.0 ** power, 2.0 ** power, unit)
     whole_steps = jnp.clip(jnp.round(weighted * (FULL / unit)[:, None]), 1.0 - FULL, FULL - 1.0)
-    ordered = dictionary.reshape(2, 4, 2, 4, 8, atoms).transpose(0, 2, 4, 1, 3, 5).reshape(512, atoms)
     vmem = pl.BlockSpec(memory_space=pltpu.VMEM)
     dma = pltpu.SemaphoreType.DMA
-    merged = pl.pallas_call(
-        functools.partial(exchange_kernel, nx, n, cap),
-        out_shape=jax.ShapeDtypeStruct((cells, time_len), F32),
-        in_specs=[vmem] * 5, out_specs=vmem,
+    halo = (blocks + 1, blocks + 1, kt, 128)
+    ordered, v1, v2, held = pl.pallas_call(
+        functools.partial(main_kernel, ni, nx, cap),
+        out_shape=(jax.ShapeDtypeStruct(dictionary.shape, BF16),
+                   jax.ShapeDtypeStruct(halo, BF16), jax.ShapeDtypeStruct(halo, BF16),
+                   jax.ShapeDtypeStruct(base_volume.shape, F32)),
+        in_specs=[vmem] * 6, out_specs=(vmem,) * 4,
         scratch_shapes=[
+            pltpu.VMEM((cells, time_len), F32),
             pltpu.VMEM((traces, 2 * time_len), BF16), pltpu.VMEM((n, traces), F32),
             pltpu.VMEM((256, traces), BF16), pltpu.VMEM((n * cap // 256, 2, 256), F32),
             pltpu.VMEM((n, 2, 256), F32), pltpu.VMEM((n, cap, time_len), WIRE),
             pltpu.VMEM((n, cap, time_len), WIRE), pltpu.VMEM((cells, time_len), F32),
             pltpu.VMEM((cells, 256), F32), pltpu.VMEM((cells, time_len), F32),
             pltpu.VMEM((256 // cap, 256, 256), BF16),
-            dma, dma((n,)), dma, dma((n,))],
-        compiler_params=pltpu.CompilerParams(collective_id=0, has_side_effects=True,
-                                             vmem_limit_bytes=40 << 20),
-        name="exchange",
-    )(whole_steps, dest_device.reshape(1, traces), dest_slot.reshape(1, traces), unit.reshape(1, traces), base_volume)
-    halo = (blocks + 1, blocks + 1, kt, 128)
-    v1, v2, residual = pl.pallas_call(
-        functools.partial(ista_kernel, ni, nx),
-        out_shape=(jax.ShapeDtypeStruct(halo, BF16), jax.ShapeDtypeStruct(halo, BF16),
-                   jax.ShapeDtypeStruct(base_volume.shape, F32)),
-        in_specs=[vmem] * 2, out_specs=(vmem,) * 3,
-        scratch_shapes=[
+            dma, dma((n,)), dma, dma((n,)),
             pltpu.VMEM((cells // 128, time_len + 8, 128), F32), pltpu.VMEM((blocks * blocks, kt, 128), F32),
             pltpu.VMEM(halo, F32), pltpu.VMEM((2 * blocks + 1, kt, 128), BF16),
             pltpu.VMEM((blocks, kt, 128), BF16), pltpu.VMEM((blocks, kt, 128), BF16),
             pltpu.VMEM((kt, 128), BF16), dma((3, 3)), dma((3, 3))],
-        compiler_params=pltpu.CompilerParams(collective_id=1, has_side_effects=True,
+        compiler_params=pltpu.CompilerParams(collective_id=0, has_side_effects=True,
                                              vmem_limit_bytes=40 << 20),
-        name="ista",
-    )(merged, ordered)
+        name="merge_and_iterate",
+    )(whole_steps, dest_device.reshape(1, traces), dest_slot.reshape(1, traces), unit.reshape(1, traces),
+      base_volume, dictionary)
+    slab = pl.BlockSpec((4, side, time_len), lambda i: (i, 0, 0))
     whole = lambda *shape: pl.BlockSpec(shape, lambda i: (0,) * len(shape))
-    codes = pl.pallas_call(
+    codes, residual = pl.pallas_call(
         codes_kernel,
         grid=(blocks,),
-        out_shape=jax.ShapeDtypeStruct((blocks, blocks, kt, atoms), F32),
-        in_specs=[whole(*halo), whole(*halo), whole(512, atoms)],
-        out_specs=pl.BlockSpec((1, blocks, kt, atoms), lambda i: (i, 0, 0, 0)),
+        out_shape=(jax.ShapeDtypeStruct((blocks, blocks, kt, atoms), F32),
+                   jax.ShapeDtypeStruct(base_volume.shape, F32)),
+        in_specs=[whole(*halo), whole(*halo), whole(512, atoms), slab],
+        out_specs=(pl.BlockSpec((1, blocks, kt, atoms), lambda i: (i, 0, 0, 0)), slab),
         compiler_params=pltpu.CompilerParams(vmem_limit_bytes=40 << 20),
         name="codes",
-    )(v1, v2, ordered)
+    )(v1, v2, ordered, held)
     return codes, residual
 
 

time: 57.3 us -> 55.2 us (0.963); the launches traced: 56.5 us -> 55 us
  local copies, waits for them, and re-layouts: 2.2 us -> 0.02 us
  other arithmetic: 2.92 us -> 4.12 us
    reshape x2 -> x0, local copies, waits for them, and re-layouts: 1.48 us -> none  [body(): dictionary.reshape(2, 4, 2, 4, 8, atoms).transpose(0, 2, 4, 1, 3, 5)]
    min x1, other arithmetic: 0.34 us -> 1.56 us  [body(): jnp.clip(jnp.round(weighted * (FULL / unit)[:, None]), 1.0 - FULL, FULL -...]
    unnamed x9 -> x8, local copies, waits for them, and re-layouts: 0.73 us -> 0.02 us
    pallas_call x3 -> x2, Pallas kernels: 50.6 us -> 50.1 us  [the longest x1 47.2 us: body(): pl.pallas_call(functools.partial(main_kernel, ni, nx, cap), out_shape=(ja...]
where the time goes in v2:
time: 55.2 us; the launch traced here: 55 us
  Pallas kernels  50.1 us (91%)
  other arithmetic  4.12 us (7%)
  between operations  0.73 us (1%)
    pallas_call x1, Pallas kernels, body(): pl.pallas_call(functools.partial(main_kernel, ni, nx, cap), out_shape=(ja...  47.2 us
    pallas_call x1, Pallas kernels, body(): pl.pallas_call(codes_kernel, grid=(blocks,), out_shape=(jax.ShapeDtypeStr...  2.95 us
    reduce_max x1, other arithmetic, body(): largest = jnp.max(jnp.abs(weighted), axis=1)  1.59 us
    min x1, other arithmetic, body(): jnp.clip(jnp.round(weighted * (FULL / unit)[:, None]), 1.0 - FULL, FULL -...  1.56 us

profile of v2, /device:TPU:3, one launch (start us, length us, event | category | flops | bytes accessed | tf_op | source)
XLA Modules:
  0.0 55.0 jit_solution(5663155113433795973)
XLA Ops:
  0.6 0.0 copy-start
  0.6 0.0 copy-start.3
  0.7 0.0 copy-start.2
  0.7 0.0 copy-start.1
  0.7 0.9 %select_reduce_fusion = f32[1024]{0:T(1024)S(1)} fusion(f32[4]{0:T(128)} %param.12, s32[1024]{0:T(1024)} %param.11), kind=kLoop, calls=%fused_computation.2 | loop fusion | flops 11264 | bytes 8208 | tf_op jit(solution)/shard_map/reduce_sum | solution.py:333
  1.5 1.6 %abs_reduce_fusion = f32[1024]{0:T(1024)S(1)} fusion(f32[1024,256]{1,0:T(8,128)} %param.8, f32[1024]{0:T(1024)S(1)} %select_reduce_fusion), kind=kLoop, calls=%fused_computation.1 | loop fusion | flops 785408 | bytes 1056768 | tf_op jit(solution)/shard_map/reduce_max | solution.py:335
  3.2 0.1 reshape_select_fusion.18.unit_ref
  3.3 1.6 %round-nearest-even_clamp_fusion.w_ref = f32[1024,256]{1,0:T(8,128)S(1)} fusion(f32[1024,256]{1,0:T(8,128)} %param.8, f32[1024]{0:T(1024)S(1)} %get-tuple-element.10, f32[1024]{0:T(1024)S(1)} %select_reduce_fusion), kind=kLoop, calls=%fused_computation | loop fusion | flops 1048576 | bytes 2105344 | tf_op jit(solution)/shard_map/jit(clip)/min | solution.py:339
  4.8 0.0 copy-done
  4.8 0.0 copy-done.3
  4.8 0.0 copy-done.2
  4.9 0.0 copy-done.1
  4.9 47.2 %merge_and_iterate.1 = (bf16[512,512]{1,0:T(8,128)(2,1)S(1)}, bf16[5,5,64,128]{3,2,1,0:T(8,128)(2,1)S(1)}, bf16[5,5,64,128]{3,2,1,0:T(8,128)(2,1)S(1)}, f32[16,16,256]{2,1,0:T(8,128)S(1)}) custom-call(f32[1024,256]{1,0:T(8,128)S(1)} %round-nearest-even_clamp_fusion.w_ref, s32[1,1024]{1,0:T(1,128)S(1)} %bitcast.3, s32[1,1024]{1,0:T(1,128)S(1)} %bitcast.4, ...), custom_call_target="tpu_custom_call" | custom-call | tf_op jit(solution)/shard_map/merge_and_iterate/pallas_call | solution.py:343
  52.0 3.0 %codes.1 = (f32[4,4,64,512]{3,2,1,0:T(8,128)}, f32[16,16,256]{2,1,0:T(8,128)}) custom-call(bf16[5,5,64,128]{3,2,1,0:T(8,128)(2,1)S(1)} %get-tuple-element.6.v1_ref, bf16[5,5,64,128]{3,2,1,0:T(8,128)(2,1)S(1)} %get-tuple-element.7.v2_ref, bf16[512,512]{1,0:T(8,128)(2,1)S(1)} %get-tuple-element.8.d_ref, f32[16,16,256]{2,1,0:T(8,128)S(1)} %get-tuple-element.9.held_ref), custom_call_target="tpu_custom_call" | custom-call | tf_op jit(solution)/shard_map/codes/pallas_call | solution.py:369
  (1 shorter events, 0.0 us)
Async XLA Ops:
  0.6 4.2 %copy-start = (bf16[512,512]{1,0:T(8,128)(2,1)S(1)}, bf16[512,512]{1,0:T(8,128)(2,1)}, u32[]{:S(2)}) copy-start(bf16[512,512]{1,0:T(8,128)(2,1)} %d_in.1) | copy-start | bytes 1572868
  0.6 4.2 %copy-start.3 = (s32[1024]{0:T(1024)S(1)}, s32[1024]{0:T(1024)}, u32[]{:S(2)}) copy-start(s32[1024]{0:T(1024)} %param.10) | copy-start | bytes 12292
  0.7 4.2 %copy-start.2 = (s32[1024,1]{0,1:T(1,128)S(1)}, s32[1024,1]{0,1:T(1,128)}, u32[]{:S(2)}) copy-start(s32[1024,1]{0,1:T(1,128)} %param.9) | copy-start | bytes 12292
  0.7 4.2 %copy-start.1 = (f32[16,16,256]{2,1,0:T(8,128)S(1)}, f32[16,16,256]{2,1,0:T(8,128)}, u32[]{:S(2)}) copy-start(f32[16,16,256]{2,1,0:T(8,128)} %base_ref.1) | copy-start | bytes 786436

commit v3 on v2

--- a/solution.py
+++ b/solution.py
@@ -78,7 +78,8 @@
 
     @pl.loop(0, chunks)
     def _(step):
-        ch = (me // q + 1 + step) % chunks
+        off = (2 * step + 1) % chunks + (2 * step + 1) // chunks
+        ch = (me // q + off) % chunks
         want = iota((cap, traces), 0).astype(F32)
         for i in range(q):
             row = rank[pl.ds(ch * q + i, 1), :]
@@ -121,7 +122,8 @@
 
     @pl.loop(0, chunks)
     def _(step):
-        ch = (me // q + chunks - 1 - step + chunks) % chunks
+        off = (2 * step + 1) % chunks + (2 * step + 1) // chunks
+        ch = (me // q + 2 * chunks - off) % chunks
         names = jnp.zeros((16, 256), F32)
         for i in range(q):
             src = ch * q + i

time: 55.2 us -> 57.5 us (1.042)
  Pallas kernels: 50.1 us -> 52.4 us
    pallas_call x1, Pallas kernels: 47.2 us -> 49.5 us  [body(): pl.pallas_call(functools.partial(main_kernel, ni, nx, cap), out_shape=(ja...]
where the time goes in v3:
time: 57.5 us; the launch traced here: 57.3 us
  Pallas kernels  52.4 us (91%)
  other arithmetic  4.12 us (7%)
  between operations  0.73 us (1%)
    pallas_call x1, Pallas kernels, body(): pl.pallas_call(functools.partial(main_kernel, ni, nx, cap), out_shape=(ja...  49.5 us
    pallas_call x1, Pallas kernels, body(): pl.pallas_call(codes_kernel, grid=(blocks,), out_shape=(jax.ShapeDtypeStr...  2.95 us
    reduce_max x1, other arithmetic, body(): largest = jnp.max(jnp.abs(weighted), axis=1)  1.59 us
    min x1, other arithmetic, body(): jnp.clip(jnp.round(weighted * (FULL / unit)[:, None]), 1.0 - FULL, FULL -...  1.56 us

profile of v3, /device:TPU:3, one launch (start us, length us, event | category | flops | bytes accessed | tf_op | source)
XLA Modules:
  0.0 57.3 jit_solution(2218667387101707886)
XLA Ops:
  0.6 0.0 copy-start
  0.6 0.0 copy-start.3
  0.7 0.0 copy-start.2
  0.7 0.0 copy-start.1
  0.7 0.9 %select_reduce_fusion = f32[1024]{0:T(1024)S(1)} fusion(f32[4]{0:T(128)} %param.12, s32[1024]{0:T(1024)} %param.11), kind=kLoop, calls=%fused_computation.2 | loop fusion | flops 11264 | bytes 8208 | tf_op jit(solution)/shard_map/reduce_sum | solution.py:335
  1.5 1.6 %abs_reduce_fusion = f32[1024]{0:T(1024)S(1)} fusion(f32[1024,256]{1,0:T(8,128)} %param.8, f32[1024]{0:T(1024)S(1)} %select_reduce_fusion), kind=kLoop, calls=%fused_computation.1 | loop fusion | flops 785408 | bytes 1056768 | tf_op jit(solution)/shard_map/reduce_max | solution.py:337
  3.2 0.1 reshape_select_fusion.18.unit_ref
  3.3 1.6 %round-nearest-even_clamp_fusion.w_ref = f32[1024,256]{1,0:T(8,128)S(1)} fusion(f32[1024,256]{1,0:T(8,128)} %param.8, f32[1024]{0:T(1024)S(1)} %get-tuple-element.10, f32[1024]{0:T(1024)S(1)} %select_reduce_fusion), kind=kLoop, calls=%fused_computation | loop fusion | flops 1048576 | bytes 2105344 | tf_op jit(solution)/shard_map/jit(clip)/min | solution.py:341
  4.8 0.0 copy-done
  4.8 0.0 copy-done.3
  4.8 0.0 copy-done.2
  4.9 0.0 copy-done.1
  4.9 49.5 %merge_and_iterate.1 = (bf16[512,512]{1,0:T(8,128)(2,1)S(1)}, bf16[5,5,64,128]{3,2,1,0:T(8,128)(2,1)S(1)}, bf16[5,5,64,128]{3,2,1,0:T(8,128)(2,1)S(1)}, f32[16,16,256]{2,1,0:T(8,128)S(1)}) custom-call(f32[1024,256]{1,0:T(8,128)S(1)} %round-nearest-even_clamp_fusion.w_ref, s32[1,1024]{1,0:T(1,128)S(1)} %bitcast.3, s32[1,1024]{1,0:T(1,128)S(1)} %bitcast.4, ...), custom_call_target="tpu_custom_call" | custom-call | tf_op jit(solution)/shard_map/merge_and_iterate/pallas_call | solution.py:345
  54.3 3.0 %codes.1 = (f32[4,4,64,512]{3,2,1,0:T(8,128)}, f32[16,16,256]{2,1,0:T(8,128)}) custom-call(bf16[5,5,64,128]{3,2,1,0:T(8,128)(2,1)S(1)} %get-tuple-element.6.v1_ref, bf16[5,5,64,128]{3,2,1,0:T(8,128)(2,1)S(1)} %get-tuple-element.7.v2_ref, bf16[512,512]{1,0:T(8,128)(2,1)S(1)} %get-tuple-element.8.d_ref, f32[16,16,256]{2,1,0:T(8,128)S(1)} %get-tuple-element.9.held_ref), custom_call_target="tpu_custom_call" | custom-call | tf_op jit(solution)/shard_map/codes/pallas_call | solution.py:371
  (1 shorter events, 0.0 us)
Async XLA Ops:
  0.6 4.2 %copy-start = (bf16[512,512]{1,0:T(8,128)(2,1)S(1)}, bf16[512,512]{1,0:T(8,128)(2,1)}, u32[]{:S(2)}) copy-start(bf16[512,512]{1,0:T(8,128)(2,1)} %d_in.1) | copy-start | bytes 1572868
  0.6 4.2 %copy-start.3 = (s32[1024]{0:T(1024)S(1)}, s32[1024]{0:T(1024)}, u32[]{:S(2)}) copy-start(s32[1024]{0:T(1024)} %param.10) | copy-start | bytes 12292
  0.7 4.2 %copy-start.2 = (s32[1024,1]{0,1:T(1,128)S(1)}, s32[1024,1]{0,1:T(1,128)}, u32[]{:S(2)}) copy-start(s32[1024,1]{0,1:T(1,128)} %param.9) | copy-start | bytes 12292
  0.7 4.2 %copy-start.1 = (f32[16,16,256]{2,1,0:T(8,128)S(1)}, f32[16,16,256]{2,1,0:T(8,128)}, u32[]{:S(2)}) copy-start(f32[16,16,256]{2,1,0:T(8,128)} %base_ref.1) | copy-start | bytes 786436
